TPU v7x, 256 devices: a whole 4x4x8 slice. The times are simulated.
256 devices in a mesh: seq: 32 (over x, z), fsdp: 8 (over y, core).
Axes of the slice: x: 4, y: 4, z: 8, core: 2. Of those that a mesh axis runs over, the one named last changes fastest.
Arguments:
- frames: bfloat16 [8, 4096, 1536], P('fsdp', 'seq'), may hold values from -6 to 6
- lengths: int32 [8, 4], P('fsdp'), may hold values from 1 to 2048, 4096 in all within a row
- offsets: int32 [8, 33], P('fsdp'), may hold values from 0 to 4096, as said below
- w_in: bfloat16 [1536, 3072], P('fsdp'), may hold values from -0.15625 to 0.15625
- kernel: float32 [31, 1536], replicated, may hold values from -1 to 1
- cotangent: bfloat16 [8, 8192, 1536], P('fsdp', 'seq'), may hold values from -6 to 6
Outputs:
- owner_output: bfloat16 [8, 8192, 1536], P('fsdp', 'seq')
- frame_grad: bfloat16 [8, 4096, 1536], P('fsdp', 'seq')
- w_grad: float32 [1536, 3072], P(('seq', 'fsdp'))
Inputs may be any that keep to these rules, and one draw needn't show every extreme that they name: Row g: device i of seq owns the frames offsets[g, i] to offsets[g, i + 1] - 1; offsets[g, 0] = 0 and offsets[g, 32] = 4096; each device owns 128 // 4 to 256 frames, beginning within 64 of i * 128; in every group one device owns exactly 256. `lengths`: each row sums to 4096; its largest entry is exactly 2048.
All inputs are finite; a program needn't handle non-finite values.
Results may differ from a plain program's by a relative error of at most 0.025.
Values may be sent and summed in bfloat16 or wider, within the bound.
No kernel may reach another device: no remote copies, remote signals or barrier semaphores. Data moves between devices by JAX's collectives and lax.ppermute only.
A program may use at most 128 MiB of HBM per device.

v0:
```python
import math
import jax
import jax.numpy as jnp
from jax import lax
from jax.sharding import PartitionSpec as P

epsilon = 1e-05


def passed_along(value, axis, steps):
    count = lax.axis_size(axis)
    initial, last = (max(0, -steps), min(count, count - steps))
    return lax.ppermute(value, axis, [(source, source + steps) for source in range(initial, last)])


def normalize_rows(values):
    values = values.astype(jnp.float32)
    center = jnp.mean(values, axis=-1, keepdims=True)
    shifted = values - center
    scale_inv = lax.rsqrt(jnp.mean(shifted * shifted, axis=-1, keepdims=True) + epsilon)
    return (shifted * scale_inv, scale_inv)


def norm_backward(upstream, normed, scale_inv):
    first_mean = jnp.mean(upstream, axis=-1, keepdims=True)
    second_mean = jnp.mean(upstream * normed, axis=-1, keepdims=True)
    return scale_inv * (upstream - first_mean - normed * second_mean)


def depthwise(window, kernel, labels, row_count):
    tap_count = kernel.shape[0]
    half_width = tap_count // 2
    centre = labels[half_width : half_width + row_count]
    result = jnp.zeros((row_count, kernel.shape[1]), jnp.float32)
    for tap_index in range(tap_count):
        same_utt = (labels[tap_index : tap_index + row_count] == centre).astype(jnp.float32)
        result = (
            result
            + kernel[tap_index]
            * window[tap_index : tap_index + row_count].astype(jnp.float32)
            * same_utt[:, None]
        )
    return result


def depthwise_back(window, kernel, labels, row_count):
    tap_count = kernel.shape[0]
    half_width = tap_count // 2
    centre = labels[half_width : half_width + row_count]
    result = jnp.zeros((row_count, kernel.shape[1]), jnp.float32)
    for tap_index in range(tap_count):
        tap_row = 2 * half_width - tap_index
        same_utt = (labels[tap_row : tap_row + row_count] == centre).astype(jnp.float32)
        result = (
            result + kernel[tap_index] * window[tap_row : tap_row + row_count] * same_utt[:, None]
        )
    return result


def finish(d_glu, values, gates, hidden, normed, scale_inv, backward_product):
    d_mixed = jnp.concatenate(
        [d_glu * gates, d_glu * values * gates * (1.0 - gates)], axis=1
    ).astype(jnp.bfloat16)
    d_hidden = backward_product(d_mixed)
    d_rows = norm_backward(d_hidden, normed, scale_inv).astype(jnp.bfloat16)
    partial_sum = lax.dot_general(
        hidden, d_mixed, (((0,), (0,)), ((), ())), preferred_element_type=jnp.float32
    )
    return (d_rows, partial_sum)


def on_device(frames, lengths, offsets, w_in, kernel, cotangent):
    rows_in = frames[0]
    per_device = rows_in.shape[0]
    model_width = rows_in.shape[1]
    capacity = 2 * per_device
    seq_count = lax.axis_size("seq")
    group_count = lax.axis_size("fsdp")
    device = lax.axis_index("seq")
    frame_total = seq_count * per_device
    half_width = kernel.shape[0] // 2
    bounds_row = offsets[0]
    start_row = bounds_row[device]
    owned_load = bounds_row[device + 1] - start_row
    base_row = (device - 1) * per_device
    utt_bounds = jnp.cumsum(lengths[0])[:-1]
    slot_index = jnp.arange(capacity, dtype=jnp.int32)
    owned = (slot_index < owned_load)[:, None]
    bf_zero = jnp.zeros((), jnp.bfloat16)
    cot_rows = jnp.where(owned, cotangent[0], bf_zero)

    def backward_product(d_mixed):
        return lax.dot_general(
            d_mixed,
            lax.all_gather(w_in, "fsdp", axis=0, tiled=True),
            (((1,), (1,)), ((), ())),
            preferred_element_type=jnp.float32,
        )

    from_prev = passed_along(rows_in, "seq", 1)
    from_next = passed_along(rows_in, "seq", -1)
    gathered = jnp.concatenate([from_prev, rows_in, from_next, jnp.zeros_like(rows_in)], axis=0)
    window_rows = capacity + 2 * half_width
    rows_window = lax.dynamic_slice_in_dim(
        gathered, start_row - half_width - base_row, window_rows, 0
    )
    positions = start_row - half_width + jnp.arange(window_rows, dtype=jnp.int32)
    labels = jnp.sum((positions[:, None] >= utt_bounds[None, :]).astype(jnp.int32), axis=1)
    inside = (positions >= 0) & (positions < frame_total)
    labels = jnp.where(inside, labels, -1)
    normed, scale_inv = normalize_rows(rows_window)
    hidden = normed.astype(jnp.bfloat16)
    projected = jnp.dot(
        hidden, lax.all_gather(w_in, "fsdp", axis=0, tiled=True), preferred_element_type=jnp.float32
    )
    values = projected[:, :model_width]
    gates = jax.nn.sigmoid(projected[:, model_width:])
    glu_out = (values * gates).astype(jnp.bfloat16)
    conv = depthwise(glu_out, kernel, labels, capacity)
    conv_normed, conv_inv = normalize_rows(conv)
    gate_out = jax.nn.sigmoid(conv_normed)
    output = conv_normed * gate_out
    owner_output = jnp.where(owned, output.astype(jnp.bfloat16), bf_zero)
    upstream = cot_rows.astype(jnp.float32)
    d_normed = upstream * (gate_out + output * (1.0 - gate_out))
    d_conv = jnp.where(owned, norm_backward(d_normed, conv_normed, conv_inv), 0.0)
    tail_rows = lax.dynamic_slice_in_dim(d_conv, owned_load - half_width, half_width, 0)
    head_rows = d_conv[:half_width]
    left_part = passed_along(tail_rows.astype(jnp.bfloat16), "seq", 1).astype(tail_rows.dtype)
    right_part = passed_along(head_rows.astype(jnp.bfloat16), "seq", -1).astype(head_rows.dtype)
    edge_zeros = jnp.zeros((half_width, model_width), jnp.float32)
    d_window = jnp.concatenate([left_part, d_conv, edge_zeros], axis=0)
    right_placed = lax.dynamic_update_slice_in_dim(
        jnp.zeros((window_rows, model_width), jnp.float32), right_part, half_width + owned_load, 0
    )
    d_window = d_window + right_placed
    d_glu = jnp.where(owned, depthwise_back(d_window, kernel, labels, capacity), 0.0)
    inner_end = half_width + capacity
    d_rows, partial_sum = finish(
        d_glu,
        values[half_width:inner_end],
        gates[half_width:inner_end],
        hidden[half_width:inner_end],
        normed[half_width:inner_end],
        scale_inv[half_width:inner_end],
        backward_product,
    )
    placed = lax.dynamic_update_slice_in_dim(
        jnp.zeros((4 * per_device, model_width), jnp.bfloat16), d_rows, start_row - base_row, 0
    )
    back_prev = passed_along(placed[:per_device], "seq", -1)
    back_next = passed_along(placed[2 * per_device : 3 * per_device], "seq", 1)
    frame_grad = (
        placed[per_device : 2 * per_device].astype(jnp.float32)
        + back_prev.astype(jnp.float32)
        + back_next.astype(jnp.float32)
    ).astype(jnp.bfloat16)
    rounded = lax.optimization_barrier(partial_sum.astype(jnp.bfloat16)).astype(jnp.float32)
    seq_summed = lax.psum_scatter(
        rounded.astype(jnp.bfloat16), "seq", scatter_dimension=0, tiled=True
    )
    summed = lax.psum_scatter(seq_summed, "fsdp", scatter_dimension=0, tiled=True).astype(
        jnp.float32
    )
    w_grad = summed * (1.0 / math.sqrt(group_count * frame_total))
    return (owner_output[None], frame_grad[None], w_grad)


def solution(mesh):
    return jax.shard_map(
        on_device,
        mesh=mesh,
        in_specs=(
            P("fsdp", "seq", None),
            P("fsdp", None),
            P("fsdp", None),
            P("fsdp", None),
            P(),
            P("fsdp", "seq", None),
        ),
        out_specs=(P("fsdp", "seq", None), P("fsdp", "seq", None), P(("seq", "fsdp"), None)),
        check_vma=False,
    )
```

profile of v0, /device:TPU:8, one launch (start us, length us, event | category | flops | bytes accessed | tf_op | source)
XLA Modules:
  0.0 391.4 jit_solution(15712493318630391508)
XLA Ops:
  8.0 3.8 collective-permute-start
  17.6 1.6 slice_reduce_fusion.29
  20.8 1.8 slice_reduce_fusion.30
  26.0 1.5 fusion.1
  27.6 41.1 %all-gather.2.cloned.1.call-done = bf16[1536,3072]{1,0:T(8,128)(2,1)} async-done(((bf16[192,3072]{1,0:T(8,128)(2,1)}), bf16[1536,3072]{1,0:T(8,128)(2,1)}) %all-gather.2.cloned.1.call-update) | async-done | bytes 9437200 | tf_op jit(solution)/shard_map/all_gather | solution.py:114
  68.7 5.4 %fusion.90 = f32[286,3072]{1,0:T(8,128)S(1)} fusion(bf16[286,1536]{1,0:T(8,128)(2,1)S(1)} %get-tuple-element.52, bf16[1536,3072]{1,0:T(8,128)(2,1)} %all-gather.2.cloned.1.call-done), kind=kOutput, calls=%fused_computation.223 | convolution fusion | flops 2699034624 | bytes 13830144 | tf_op jit(solution)/shard_map/dot_general | solution.py:113
  74.2 2.1 fusion.6
  76.9 13.3 %fusion.86 = (f32[256]{0:T(256)S(1)}, f32[256,1536]{1,0:T(8,128)S(1)}) fusion(f32[256]{0:T(256)S(1)} %get-tuple-element.82, bf16[286,1536]{1,0:T(8,128)(2,1)S(1)} %get-tuple-element.46, f32[1536]{0:T(1024)S(1)} %get-tuple-element.36, f32[256]{0:T(256)S(1)} %get-tuple-element.54, f32[1536]{0:T(1024)S(1)} %get-tuple-element.37, f32[256]{0:T(256)S(1)} %get-tuple-element.55, ...), kind=kLoop, calls=%fused_computation.220 | loop fusion | flops 48365312 | bytes 26174464 | tf_op jit(solution)/shard_map/reduce_sum | solution.py:18
  91.3 1.7 fusion.84
  95.3 3.5 collective-permute-start.2
  101.0 1.6 maximum_maximum_fusion
  102.6 2.9 collective-permute-done.3
  106.2 10.6 %multiply_convert_fusion.1 = (bf16[256,1536]{1,0:T(8,128)(2,1)S(1)}, f32[256,1536]{1,0:T(8,128)S(1)}) fusion(f32[286,1536]{1,0:T(8,128)} %get-tuple-element.45, f32[256]{0:T(256)} %copy-done.37, f32[286,1536]{1,0:T(8,128)S(1)} %add.319, f32[1536]{0:T(1024)} %copy-done.26, f32[256]{0:T(256)} %copy-done.46, f32[1536]{0:T(1024)} %copy-done.27, ...), kind=kLoop, calls=%fused_computation.115 | loop fusion | flops 36962304 | bytes 52912384 | tf_op jit(solution)/shard_map/convert
  116.9 2.3 fusion.10
  120.0 5.2 %convolution_convert_fusion = bf16[1536,3072]{1,0:T(8,128)(2,1)} fusion(bf16[256,1536]{1,0:T(8,128)(2,1)S(1)} %fusion.10, bf16[256,1536]{1,0:T(8,128)(2,1)S(1)} %get-tuple-element.38, bf16[286,1536]{1,0:T(8,128)(2,1)S(1)} %copy-done.6), kind=kOutput, calls=%fused_computation | convolution fusion | flops 2423783424 | bytes 11796480 | tf_op jit(solution)/shard_map/dot_general | solution.py:66
  127.5 2.1 select_bitcast_fusion
  129.5 5.9 %fusion.83 = (f32[256]{0:T(256)S(1)}, f32[256]{0:T(256)S(1)}, f32[256,1536]{1,0:T(8,128)S(1)}) fusion(f32[286,1536]{1,0:T(8,128)S(1)} %copy-done.3, bf16[1536,3072]{1,0:T(8,128)(2,1)} %all-gather.2.cloned.1.call-done, bf16[256,1536]{1,0:T(8,128)(2,1)} %copy-done.8, bf16[256,1536]{1,0:T(8,128)(2,1)} %copy-done.9), kind=kOutput, calls=%fused_computation.218 | convolution fusion | flops 2420243968 | bytes 14157824 | tf_op jit(solution)/shard_map/dot_general | solution.py:93
  137.9 4.0 %dynamic_update_slice.7 = bf16[512,1536]{1,0:T(8,128)(2,1)S(1)} dynamic-update-slice(bf16[512,1536]{1,0:T(8,128)(2,1)S(1)} %broadcast_in_dim.45, bf16[256,1536]{1,0:T(8,128)(2,1)S(1)} %copy-done.4, s32[]{:T(128)S(6)} %select_n.46, s32[]{:T(128)} %constant.22.clone.1) | dynamic-update-slice | bytes 1572868 | tf_op jit(solution)/shard_map/dynamic_update_slice | solution.py:148
  143.2 4.6 %collective-permute-start.5 = (bf16[128,1536]{1,0:T(8,128)(2,1)S(1)}, bf16[128,1536]{1,0:T(8,128)(2,1)S(1)}, u32[]{:S(2)}, u32[]{:S(2)}) collective-permute-start(bf16[128,1536]{1,0:T(8,128)(2,1)S(1)} %get-tuple-element.48), channel_id=1, source_target_pairs={{0,8},{8,16},{16,24},{24,32},{32,40},{40,48},{48,56},{56,64},{64,7... | collective-permute-start | bytes 1179656 | tf_op jit(solution)/shard_map/ppermute | solution.py:13
  147.8 212.4 %reduce-scatter.4.cloned.1.call-done = bf16[48,3072]{1,0:T(8,128)(2,1)} async-done(((bf16[1536,3072]{1,0:T(8,128)(2,1)}), bf16[48,3072]{1,0:T(8,128)(2,1)}) %reduce-scatter.4.cloned.1.call-update) | async-done | bytes 294928 | tf_op jit(solution)/shard_map/reduce_scatter | solution.py:159
  360.2 14.8 %fusion = bf16[8,3072]{1,0:T(8,128)(2,1)S(1)} fusion(bf16[48,3072]{1,0:T(8,128)(2,1)} %reduce-scatter.4.cloned.1.call-done), kind=kCustom, calls=%all-reduce-scatter | all-reduce-scatter fusion | flops 196609 | bytes 345088
  375.0 1.9 collective-permute-start.6
  376.9 2.1 collective-permute-start.7
  379.9 3.6 collective-permute-done.7
  (160 shorter events, 23.1 us)
Async XLA Ops:
  7.2 61.5 %all-gather.2.cloned.1.call-start = ((), (), s32[]{:S(2)}) async-start(), calls=%async_computation.1 | async-start | bytes 10616832 | tf_op jit(solution)/shard_map/all_gather | solution.py:114
  7.9 352.3 %reduce-scatter.4.cloned.1.call-start = ((), (), s32[]{:S(2)}) async-start(), calls=%async_computation.2 | async-start | bytes 9732096 | tf_op jit(solution)/shard_map/reduce_scatter | solution.py:159
  8.0 15.4 %collective-permute-start = (bf16[128,1536]{1,0:T(8,128)(2,1)}, bf16[128,1536]{1,0:T(8,128)(2,1)S(1)}, u32[]{:S(2)}, u32[]{:S(2)}) collective-permute-start(bf16[128,1536]{1,0:T(8,128)(2,1)} %bitcast.21), channel_id=1, source_target_pairs={{0,8},{8,16},{16,24},{24,32},{32,40},{40,48},{48,56},{56,64},{64,7... | collective-permute-start | bytes 1179656 | tf_op jit(solution)/shard_map/ppermute | solution.py:13
  11.8 12.8 %collective-permute-start.1 = (bf16[128,1536]{1,0:T(8,128)(2,1)}, bf16[128,1536]{1,0:T(8,128)(2,1)S(1)}, u32[]{:S(2)}, u32[]{:S(2)}) collective-permute-start(bf16[128,1536]{1,0:T(8,128)(2,1)} %bitcast.22), channel_id=1, source_target_pairs={{8,0},{16,8},{24,16},{32,24},{40,32},{48,40},{56,48},{64,56},{72,6... | collective-permute-start | bytes 1179656 | tf_op jit(solution)/shard_map/ppermute | solution.py:13
  19.2 57.3 %copy-start.16 = (f32[1536]{0:T(1024)}, f32[1536]{0:T(1024)S(1)}, u32[]{:S(2)}) copy-start(f32[1536]{0:T(1024)S(1)} %get-tuple-element.26) | copy-start | bytes 18436
  19.2 57.3 %copy-start.17 = (f32[1536]{0:T(1024)}, f32[1536]{0:T(1024)S(1)}, u32[]{:S(2)}) copy-start(f32[1536]{0:T(1024)S(1)} %get-tuple-element.27) | copy-start | bytes 18436
  19.2 57.3 %copy-start.18 = (f32[1536]{0:T(1024)}, f32[1536]{0:T(1024)S(1)}, u32[]{:S(2)}) copy-start(f32[1536]{0:T(1024)S(1)} %get-tuple-element.28) | copy-start | bytes 18436
  19.2 57.3 %copy-start.19 = (f32[1536]{0:T(1024)}, f32[1536]{0:T(1024)S(1)}, u32[]{:S(2)}) copy-start(f32[1536]{0:T(1024)S(1)} %get-tuple-element.29) | copy-start | bytes 18436
  19.3 57.3 %copy-start.20 = (f32[1536]{0:T(1024)}, f32[1536]{0:T(1024)S(1)}, u32[]{:S(2)}) copy-start(f32[1536]{0:T(1024)S(1)} %get-tuple-element.30) | copy-start | bytes 18436
  19.3 57.3 %copy-start.21 = (f32[1536]{0:T(1024)}, f32[1536]{0:T(1024)S(1)}, u32[]{:S(2)}) copy-start(f32[1536]{0:T(1024)S(1)} %get-tuple-element.31) | copy-start | bytes 18436
  19.3 57.3 %copy-start.22 = (f32[1536]{0:T(1024)}, f32[1536]{0:T(1024)S(1)}, u32[]{:S(2)}) copy-start(f32[1536]{0:T(1024)S(1)} %get-tuple-element.32) | copy-start | bytes 18436
  19.3 57.3 %copy-start.23 = (f32[1536]{0:T(1024)}, f32[1536]{0:T(1024)S(1)}, u32[]{:S(2)}) copy-start(f32[1536]{0:T(1024)S(1)} %get-tuple-element.33) | copy-start | bytes 18436
  19.3 57.3 %copy-start.24 = (f32[1536]{0:T(1024)}, f32[1536]{0:T(1024)S(1)}, u32[]{:S(2)}) copy-start(f32[1536]{0:T(1024)S(1)} %get-tuple-element.34) | copy-start | bytes 18436
  19.3 57.3 %copy-start.25 = (f32[1536]{0:T(1024)}, f32[1536]{0:T(1024)S(1)}, u32[]{:S(2)}) copy-start(f32[1536]{0:T(1024)S(1)} %get-tuple-element.35) | copy-start | bytes 18436
  19.3 57.3 %copy-start.26 = (f32[1536]{0:T(1024)}, f32[1536]{0:T(1024)S(1)}, u32[]{:S(2)}) copy-start(f32[1536]{0:T(1024)S(1)} %get-tuple-element.36) | copy-start | bytes 18436
  19.3 57.3 %copy-start.27 = (f32[1536]{0:T(1024)}, f32[1536]{0:T(1024)S(1)}, u32[]{:S(2)}) copy-start(f32[1536]{0:T(1024)S(1)} %get-tuple-element.37) | copy-start | bytes 18436
  19.4 57.2 %copy-start.35 = (f32[256]{0:T(256)}, f32[256]{0:T(256)S(1)}, u32[]{:S(2)}) copy-start(f32[256]{0:T(256)S(1)} %get-tuple-element.81) | copy-start | bytes 3076
  19.4 57.2 %copy-start.36 = (f32[256]{0:T(256)}, f32[256]{0:T(256)S(1)}, u32[]{:S(2)}) copy-start(f32[256]{0:T(256)S(1)} %get-tuple-element.82) | copy-start | bytes 3076
  95.3 5.6 %collective-permute-start.2 = (bf16[15,1536]{1,0:T(8,128)(2,1)S(1)}, bf16[15,1536]{1,0:T(8,128)(2,1)S(1)}, u32[]{:S(2)}, u32[]{:S(2)}) collective-permute-start(bf16[15,1536]{1,0:T(8,128)(2,1)S(1)} %get-tuple-element.50), channel_id=1, source_target_pairs={{0,8},{8,16},{16,24},{24,32},{32,40},{40,48},{48,56},{56,64},{64,7... | collective-permute-start | bytes 138248 | tf_op jit(solution)/shard_map/ppermute | solution.py:13
  99.5 6.0 %collective-permute-start.3 = (bf16[15,1536]{1,0:T(8,128)(2,1)S(1)}, bf16[15,1536]{1,0:T(8,128)(2,1)S(1)}, u32[]{:S(2)}, u32[]{:S(2)}) collective-permute-start(bf16[15,1536]{1,0:T(8,128)(2,1)S(1)} %get-tuple-element.49), channel_id=1, source_target_pairs={{8,0},{16,8},{24,16},{32,24},{40,32},{48,40},{56,48},{64,56},{72,6... | collective-permute-start | bytes 138248 | tf_op jit(solution)/shard_map/ppermute | solution.py:13
  141.9 237.1 %collective-permute-start.4 = (bf16[128,1536]{1,0:T(8,128)(2,1)S(1)}, bf16[128,1536]{1,0:T(8,128)(2,1)S(1)}, u32[]{:S(2)}, u32[]{:S(2)}) collective-permute-start(bf16[128,1536]{1,0:T(8,128)(2,1)S(1)} %get-tuple-element.47), channel_id=1, source_target_pairs={{8,0},{16,8},{24,16},{32,24},{40,32},{48,40},{56,48},{64,56},{72,6... | collective-permute-start | bytes 1179656 | tf_op jit(solution)/shard_map/ppermute | solution.py:13
  143.2 235.8 %collective-permute-start.5 = (bf16[128,1536]{1,0:T(8,128)(2,1)S(1)}, bf16[128,1536]{1,0:T(8,128)(2,1)S(1)}, u32[]{:S(2)}, u32[]{:S(2)}) collective-permute-start(bf16[128,1536]{1,0:T(8,128)(2,1)S(1)} %get-tuple-element.48), channel_id=1, source_target_pairs={{0,8},{8,16},{16,24},{24,32},{32,40},{40,48},{48,56},{56,64},{64,7... | collective-permute-start | bytes 1179656 | tf_op jit(solution)/shard_map/ppermute | solution.py:13
  375.0 8.5 %collective-permute-start.6 = (bf16[8,3072]{1,0:T(8,128)(2,1)S(1)}, bf16[8,3072]{1,0:T(8,128)(2,1)S(1)}, u32[]{:S(2)}, u32[]{:S(2)}) collective-permute-start(bf16[8,3072]{1,0:T(8,128)(2,1)S(1)} %fusion), channel_id=1, source_target_pairs={{0,1},{1,2},{2,3},{3,4},{4,5},{5,6},{6,7},{8,9},{9,10},{10,11},{11... | collective-permute-start | bytes 147464
  376.9 6.6 %collective-permute-start.7 = (bf16[6,3072]{1,0:T(8,128)(2,1)S(1)}, bf16[6,3072]{1,0:T(8,128)(2,1)S(1)}, u32[]{:S(2)}, u32[]{:S(2)}) collective-permute-start(bf16[6,3072]{1,0:T(8,128)(2,1)S(1)} %slice.684), channel_id=1, source_target_pairs={{0,2},{1,3},{2,4},{3,5},{4,6},{5,7},{8,10},{9,11},{10,12},{11,13},... | collective-permute-start | bytes 110600
  (40 other events, 1343.1 us)
Sparse Core Ops, SparseCore 0:
  9.8 58.8 all-gather.1
  125.4 234.7 reduce-scatter.3
where the time goes:
time: 392 us; the launch traced here: 391 us
  waiting for transfers between devices  262 us (67%)
  other arithmetic  43.6 us (11%)
  starting transfers between devices  20 us (5%)
  between operations  18.5 us (5%)
  matrix products  16.6 us (4%)
  local copies, waits for them, and re-layouts  15.9 us (4%)
  blocking collectives  14.8 us (4%)
    reduce_scatter x1, waiting for transfers between devices, on_device(): lax.psum_scatter(rounded.astype(jnp.bfloat16), 'seq', scatter_dimension=0...  212 us
    all_gather x1, waiting for transfers between devices, on_device(): lax.all_gather(w_in, 'fsdp', axis=0, tiled=True)  41.1 us
    ppermute x6, starting transfers between devices, passed_along(): lax.ppermute(value, axis, [(source, source + steps) for source in range(i...  15.9 us
    unnamed x1, blocking collectives  14.8 us
    reduce_sum x2, other arithmetic, normalize_rows(): center = jnp.mean(values, axis=-1, keepdims=True)  14.2 us
    another operation x3, other arithmetic  13.7 us
  transfers between devices with their start and end apart: 10, of which 5 were waited for; matrix products, arithmetic and copies ran while one was open for 11% of the time, Pallas kernels for 0%

commit v1 on v0

--- a/solution.py
+++ b/solution.py
@@ -5,6 +5,35 @@
 from jax.sharding import PartitionSpec as P
 
 epsilon = 1e-05
+
+
+def surface_post(chunk, in_dim):
+    right_arr = lax.axis_size("fsdp")
+    known = lax.axis_index("fsdp")
+    part_next, now, high = (right_arr, known, chunk.shape[in_dim])
+    tray = []
+    for s in tuple(range(part_next)):
+        tray.append((s, (s + 1) % part_next))
+    ledger = []
+    for s in [*range(part_next)]:
+        ledger.append((s, (s - 1) % part_next))
+    d_next = jnp.zeros(
+        (*chunk.shape[:in_dim], part_next * high, *chunk.shape[in_dim + 1 :]), chunk.dtype
+    )
+    d_next = lax.dynamic_update_slice_in_dim(d_next, chunk, now * high, axis=in_dim)
+    moved = carry_in = chunk
+    heard = part_next // 2
+    for k0 in [*range(1, heard + 1)]:
+        moved = lax.ppermute(moved, axis_name="fsdp", perm=tray)
+        d_next = lax.dynamic_update_slice_in_dim(
+            d_next, moved, (now - k0) % part_next * high, axis=in_dim
+        )
+        if k0 < part_next - heard:
+            carry_in = lax.ppermute(carry_in, axis_name="fsdp", perm=ledger)
+            d_next = lax.dynamic_update_slice_in_dim(
+                d_next, carry_in, (now + k0) % part_next * high, axis=in_dim
+            )
+    return d_next
 
 
 def passed_along(value, axis, steps):
@@ -110,9 +139,7 @@
     labels = jnp.where(inside, labels, -1)
     normed, scale_inv = normalize_rows(rows_window)
     hidden = normed.astype(jnp.bfloat16)
-    projected = jnp.dot(
-        hidden, lax.all_gather(w_in, "fsdp", axis=0, tiled=True), preferred_element_type=jnp.float32
-    )
+    projected = jnp.dot(hidden, surface_post(w_in, in_dim=0), preferred_element_type=jnp.float32)
     values = projected[:, :model_width]
     gates = jax.nn.sigmoid(projected[:, model_width:])
     glu_out = (values * gates).astype(jnp.bfloat16)

time: 392 us -> 439 us (1.12)
  waiting for transfers between devices: 262 us -> 285 us
  local copies, waits for them, and re-layouts: 15.9 us -> 31.3 us
  starting transfers between devices: 20 us -> 26.9 us
    ppermute x0 -> x7, waiting for transfers between devices: none -> 64.2 us  [the longest x4 64.1 us: surface_post(): moved = lax.ppermute(moved, axis_name='fsdp', perm=tray)]
    all_gather x1, waiting for transfers between devices: 41.1 us -> 0.01 us  [backward_product(): lax.all_gather(w_in, 'fsdp', axis=0, tiled=True)]
    dynamic_update_slice x0 -> x8, local copies, waits for them, and re-layouts: none -> 8.99 us  [the longest x4 4.51 us: surface_post(): lax.dynamic_update_slice_in_dim(d_next, moved, (now - k0) % part_next * h...]
    ppermute x0 -> x7, starting transfers between devices: none -> 5.75 us  [the longest x3 5.7 us: surface_post(): carry_in = lax.ppermute(carry_in, axis_name='fsdp', perm=ledger)]
    broadcast_in_dim x0 -> x1, local copies, waits for them, and re-layouts: none -> 4.85 us  [surface_post(): jnp.zeros((*chunk.shape[:in_dim], part_next * high, *chunk.shape[in_dim +...]
  transfers between devices with their start and end apart: 10 -> 17, of which waited for: 5 -> 7; matrix products, arithmetic and copies ran while one was open for 11% -> 23% of each run, Pallas kernels for 0% -> 0%
where the time goes in v1:
time: 439 us; the launch traced here: 438 us
  waiting for transfers between devices  285 us (65%)
  other arithmetic  43.7 us (10%)
  local copies, waits for them, and re-layouts  31.3 us (7%)
  starting transfers between devices  26.9 us (6%)
  between operations  20.1 us (5%)
  matrix products  16.6 us (4%)
  blocking collectives  14.6 us (3%)
    reduce_scatter x1, waiting for transfers between devices, on_device(): lax.psum_scatter(rounded.astype(jnp.bfloat16), 'seq', scatter_dimension=0...  214 us
    ppermute x4, waiting for transfers between devices, surface_post(): moved = lax.ppermute(moved, axis_name='fsdp', perm=tray)  64.1 us
    ppermute x6, starting transfers between devices, passed_along(): lax.ppermute(value, axis, [(source, source + steps) for source in range(i...  16.9 us
    reduce_sum x2, other arithmetic, normalize_rows(): center = jnp.mean(values, axis=-1, keepdims=True)  15.5 us
    unnamed x1, blocking collectives  14.6 us
    another operation x3, other arithmetic  13.7 us
  transfers between devices with their start and end apart: 17, of which 7 were waited for; matrix products, arithmetic and copies ran while one was open for 23% of the time, Pallas kernels for 0%

profile of v1, /device:TPU:8, one launch (start us, length us, event | category | flops | bytes accessed | tf_op | source)
XLA Modules:
  0.0 437.9 jit_solution(10614316564241914242)
XLA Ops:
  9.8 4.6 %collective-permute-start = (bf16[128,1536]{1,0:T(8,128)(2,1)}, bf16[128,1536]{1,0:T(8,128)(2,1)}, u32[]{:S(2)}, u32[]{:S(2)}) collective-permute-start(bf16[128,1536]{1,0:T(8,128)(2,1)} %bitcast.21), channel_id=1, source_target_pairs={{0,8},{8,16},{16,24},{24,32},{32,40},{40,48},{48,56},{56,64},{64,7... | collective-permute-start | bytes 1179656 | tf_op jit(solution)/shard_map/ppermute | solution.py:42
  19.4 2.6 slice_reduce_fusion.30
  22.7 4.8 %broadcast_in_dim.44 = bf16[1536,3072]{1,0:T(8,128)(2,1)} broadcast(bf16[]{:T(256)} %constant.101.clone.1), dimensions={} | broadcast | bytes 9437186 | tf_op jit(solution)/shard_map/broadcast_in_dim | solution.py:20
  28.7 2.1 slice_reduce_fusion.29
  34.2 2.1 convert_reduce_fusion
  38.4 35.7 %collective-permute-done.4 = bf16[192,3072]{1,0:T(8,128)(2,1)S(1)} collective-permute-done((bf16[192,3072]{1,0:T(8,128)(2,1)S(1)}, bf16[192,3072]{1,0:T(8,128)(2,1)S(1)}, u32[]{:S(2)}, u32[]{:S(2)}) %collective-permute-start.4) | collective-permute-done | bytes 1179680 | tf_op jit(solution)/shard_map/ppermute | solution.py:27
  77.0 2.3 collective-permute-start.7
  80.4 17.2 %collective-permute-done.6 = bf16[192,3072]{1,0:T(8,128)(2,1)S(1)} collective-permute-done((bf16[192,3072]{1,0:T(8,128)(2,1)S(1)}, bf16[192,3072]{1,0:T(8,128)(2,1)S(1)}, u32[]{:S(2)}, u32[]{:S(2)}) %collective-permute-start.6) | collective-permute-done | bytes 1179680 | tf_op jit(solution)/shard_map/ppermute | solution.py:27
  102.1 11.2 %collective-permute-done.8 = bf16[192,3072]{1,0:T(8,128)(2,1)S(1)} collective-permute-done((bf16[192,3072]{1,0:T(8,128)(2,1)S(1)}, bf16[192,3072]{1,0:T(8,128)(2,1)S(1)}, u32[]{:S(2)}, u32[]{:S(2)}) %collective-permute-start.8) | collective-permute-done | bytes 1179680 | tf_op jit(solution)/shard_map/ppermute | solution.py:27
  114.3 5.4 %fusion.90 = f32[286,3072]{1,0:T(8,128)S(1)} fusion(bf16[286,1536]{1,0:T(8,128)(2,1)S(1)} %get-tuple-element.52, bf16[1536,3072]{1,0:T(8,128)(2,1)} %constant_dynamic-update-slice_fusion), kind=kOutput, calls=%fused_computation.231 | convolution fusion | flops 2699034624 | bytes 13830144 | tf_op jit(solution)/shard_map/dot_general | solution.py:142
  120.2 2.0 fusion.6
  122.7 13.4 %fusion.86 = (f32[256]{0:T(256)S(1)}, f32[256,1536]{1,0:T(8,128)S(1)}) fusion(f32[256]{0:T(256)S(1)} %copy-done.45, bf16[286,1536]{1,0:T(8,128)(2,1)S(1)} %get-tuple-element.46, f32[1536]{0:T(1024)S(1)} %copy-done.39, f32[256]{0:T(256)S(1)} %copy-done.47, f32[1536]{0:T(1024)S(1)} %copy-done.40, f32[256]{0:T(256)S(1)} %copy-done.48, f32[1536]{0:T(1024)S(1)} %copy-done.11, ...), kind=kLoop, calls=%fused_computation.228 | loop fusion | flops 48365312 | bytes 26174464 | tf_op jit(solution)/shard_map/reduce_sum | solution.py:47
  140.0 3.7 collective-permute-start.9
  147.5 2.9 collective-permute-done.10
  151.2 10.6 %multiply_convert_fusion.1 = (bf16[256,1536]{1,0:T(8,128)(2,1)S(1)}, f32[256,1536]{1,0:T(8,128)S(1)}) fusion(f32[286,1536]{1,0:T(8,128)} %get-tuple-element.45, f32[256]{0:T(256)} %get-tuple-element.53, f32[286,1536]{1,0:T(8,128)S(1)} %add.396, f32[1536]{0:T(1024)} %get-tuple-element.36, f32[256]{0:T(256)} %get-tuple-element.62, ...), kind=kLoop, calls=%fused_computation.115 | loop fusion | flops 36962304 | bytes 52912384 | tf_op jit(solution)/shard_map/convert
  161.8 2.3 fusion.10
  165.0 5.2 %convolution_convert_fusion = bf16[1536,3072]{1,0:T(8,128)(2,1)} fusion(bf16[256,1536]{1,0:T(8,128)(2,1)S(1)} %fusion.10, bf16[256,1536]{1,0:T(8,128)(2,1)S(1)} %get-tuple-element.38, bf16[286,1536]{1,0:T(8,128)(2,1)S(1)} %copy-done.7), kind=kOutput, calls=%fused_computation | convolution fusion | flops 2423783424 | bytes 11796480 | tf_op jit(solution)/shard_map/dot_general | solution.py:95
  173.8 5.9 %fusion.83 = (f32[256]{0:T(256)S(1)}, f32[256]{0:T(256)S(1)}, f32[256,1536]{1,0:T(8,128)S(1)}) fusion(f32[286,1536]{1,0:T(8,128)S(1)} %copy-done.3, bf16[1536,3072]{1,0:T(8,128)(2,1)} %all-gather.2.cloned.1.call-done, bf16[256,1536]{1,0:T(8,128)(2,1)} %copy-done.9, bf16[256,1536]{1,0:T(8,128)(2,1)} %copy-done.10), kind=kOutput, calls=%fused_computation.226 | convolution fusion | flops 2420243968 | bytes 14157824 | tf_op jit(solution)/shard_map/dot_general | solution.py:122
  182.2 4.0 dynamic_update_slice.39
  187.6 4.6 %collective-permute-start.12 = (bf16[128,1536]{1,0:T(8,128)(2,1)S(1)}, bf16[128,1536]{1,0:T(8,128)(2,1)S(1)}, u32[]{:S(2)}, u32[]{:S(2)}) collective-permute-start(bf16[128,1536]{1,0:T(8,128)(2,1)S(1)} %get-tuple-element.48), channel_id=1, source_target_pairs={{0,8},{8,16},{16,24},{24,32},{32,40},{40,48},{48,56},{56,64},{64,7... | collective-permute-start | bytes 1179656 | tf_op jit(solution)/shard_map/ppermute | solution.py:42
  192.1 214.1 %reduce-scatter.4.cloned.1.call-done = bf16[48,3072]{1,0:T(8,128)(2,1)} async-done(((bf16[1536,3072]{1,0:T(8,128)(2,1)}), bf16[48,3072]{1,0:T(8,128)(2,1)}) %reduce-scatter.4.cloned.1.call-update) | async-done | bytes 294928 | tf_op jit(solution)/shard_map/reduce_scatter | solution.py:186
  406.2 14.6 %fusion = bf16[8,3072]{1,0:T(8,128)(2,1)S(1)} fusion(bf16[48,3072]{1,0:T(8,128)(2,1)} %reduce-scatter.4.cloned.1.call-done), kind=kCustom, calls=%all-reduce-scatter | all-reduce-scatter fusion | flops 196609 | bytes 345088
  422.8 2.3 collective-permute-start.14
  426.0 3.4 collective-permute-done.14
  (207 shorter events, 40.9 us)
Async XLA Ops:
  8.0 165.8 %all-gather.2.cloned.1.call-start = ((), (), s32[]{:S(2)}) async-start(), calls=%async_computation.1 | async-start | bytes 10616832 | tf_op jit(solution)/shard_map/all_gather | solution.py:124
  8.0 25.4 %collective-permute-start.2 = (bf16[192,3072]{1,0:T(8,128)(2,1)}, bf16[192,3072]{1,0:T(8,128)(2,1)S(1)}, u32[]{:S(2)}, u32[]{:S(2)}) collective-permute-start(bf16[192,3072]{1,0:T(8,128)(2,1)} %param.9), channel_id=1, source_target_pairs={{0,1},{1,2},{2,3},{3,4},{4,5},{5,6},{6,7},{7,0},{8,9},{9,10},{10,1... | collective-permute-start | bytes 3538952 | tf_op jit(solution)/shard_map/ppermute | solution.py:27
  8.1 28.3 %collective-permute-start.3 = (bf16[192,3072]{1,0:T(8,128)(2,1)}, bf16[192,3072]{1,0:T(8,128)(2,1)S(1)}, u32[]{:S(2)}, u32[]{:S(2)}) collective-permute-start(bf16[192,3072]{1,0:T(8,128)(2,1)} %param.9), channel_id=1, source_target_pairs={{0,7},{1,0},{2,1},{3,2},{4,3},{5,4},{6,5},{7,6},{8,15},{9,8},{10,9... | collective-permute-start | bytes 3538952 | tf_op jit(solution)/shard_map/ppermute | solution.py:32
  9.8 24.4 %collective-permute-start = (bf16[128,1536]{1,0:T(8,128)(2,1)}, bf16[128,1536]{1,0:T(8,128)(2,1)}, u32[]{:S(2)}, u32[]{:S(2)}) collective-permute-start(bf16[128,1536]{1,0:T(8,128)(2,1)} %bitcast.21), channel_id=1, source_target_pairs={{0,8},{8,16},{16,24},{24,32},{32,40},{40,48},{48,56},{56,64},{64,7... | collective-permute-start | bytes 1179656 | tf_op jit(solution)/shard_map/ppermute | solution.py:42
  14.4 19.9 %collective-permute-start.1 = (bf16[128,1536]{1,0:T(8,128)(2,1)}, bf16[128,1536]{1,0:T(8,128)(2,1)}, u32[]{:S(2)}, u32[]{:S(2)}) collective-permute-start(bf16[128,1536]{1,0:T(8,128)(2,1)} %bitcast.22), channel_id=1, source_target_pairs={{8,0},{16,8},{24,16},{32,24},{40,32},{48,40},{56,48},{64,56},{72,6... | collective-permute-start | bytes 1179656 | tf_op jit(solution)/shard_map/ppermute | solution.py:42
  15.7 390.6 %reduce-scatter.4.cloned.1.call-start = ((), (), s32[]{:S(2)}) async-start(), calls=%async_computation.2 | async-start | bytes 9732096 | tf_op jit(solution)/shard_map/reduce_scatter | solution.py:186
  19.4 102.8 %copy-start.43 = (f32[256]{0:T(256)}, f32[256]{0:T(256)S(1)}, u32[]{:S(2)}) copy-start(f32[256]{0:T(256)S(1)} %get-tuple-element.80) | copy-start | bytes 3076
  33.4 40.7 %collective-permute-start.4 = (bf16[192,3072]{1,0:T(8,128)(2,1)S(1)}, bf16[192,3072]{1,0:T(8,128)(2,1)S(1)}, u32[]{:S(2)}, u32[]{:S(2)}) collective-permute-start(bf16[192,3072]{1,0:T(8,128)(2,1)S(1)} %collective-permute-done.2), channel_id=1, source_target_pairs={{0,1},{1,2},{2,3},{3,4},{4,5},{5,6},{6,7},{7,0},{8,9},{9,10},{10,1... | collective-permute-start | bytes 3538952 | tf_op jit(solution)/shard_map/ppermute | solution.py:27
  34.1 88.1 %copy-start.54 = (f32[256]{0:T(256)}, f32[256]{0:T(256)S(1)}, u32[]{:S(2)}) copy-start(f32[256]{0:T(256)S(1)} %get-tuple-element.71) | copy-start | bytes 3076
  34.1 88.1 %copy-start.55 = (f32[256]{0:T(256)}, f32[256]{0:T(256)S(1)}, u32[]{:S(2)}) copy-start(f32[256]{0:T(256)S(1)} %get-tuple-element.72) | copy-start | bytes 3076
  34.1 88.1 %copy-start.56 = (f32[256]{0:T(256)}, f32[256]{0:T(256)S(1)}, u32[]{:S(2)}) copy-start(f32[256]{0:T(256)S(1)} %get-tuple-element.73) | copy-start | bytes 3076
  34.2 88.1 %copy-start.57 = (f32[256]{0:T(256)}, f32[256]{0:T(256)S(1)}, u32[]{:S(2)}) copy-start(f32[256]{0:T(256)S(1)} %get-tuple-element.74) | copy-start | bytes 3076
  34.2 88.1 %copy-start.58 = (f32[256]{0:T(256)}, f32[256]{0:T(256)S(1)}, u32[]{:S(2)}) copy-start(f32[256]{0:T(256)S(1)} %get-tuple-element.75) | copy-start | bytes 3076
  34.2 88.1 %copy-start.59 = (f32[256]{0:T(256)}, f32[256]{0:T(256)S(1)}, u32[]{:S(2)}) copy-start(f32[256]{0:T(256)S(1)} %get-tuple-element.76) | copy-start | bytes 3076
  36.4 40.6 %collective-permute-start.5 = (bf16[192,3072]{1,0:T(8,128)(2,1)S(1)}, bf16[192,3072]{1,0:T(8,128)(2,1)S(1)}, u32[]{:S(2)}, u32[]{:S(2)}) collective-permute-start(bf16[192,3072]{1,0:T(8,128)(2,1)S(1)} %collective-permute-done.3), channel_id=1, source_target_pairs={{0,7},{1,0},{2,1},{3,2},{4,3},{5,4},{6,5},{7,6},{8,15},{9,8},{10,9... | collective-permute-start | bytes 3538952 | tf_op jit(solution)/shard_map/ppermute | solution.py:32
  74.2 23.4 %collective-permute-start.6 = (bf16[192,3072]{1,0:T(8,128)(2,1)S(1)}, bf16[192,3072]{1,0:T(8,128)(2,1)S(1)}, u32[]{:S(2)}, u32[]{:S(2)}) collective-permute-start(bf16[192,3072]{1,0:T(8,128)(2,1)S(1)} %collective-permute-done.4), channel_id=1, source_target_pairs={{0,1},{1,2},{2,3},{3,4},{4,5},{5,6},{6,7},{7,0},{8,9},{9,10},{10,1... | collective-permute-start | bytes 3538952 | tf_op jit(solution)/shard_map/ppermute | solution.py:27
  77.0 23.9 %collective-permute-start.7 = (bf16[192,3072]{1,0:T(8,128)(2,1)S(1)}, bf16[192,3072]{1,0:T(8,128)(2,1)S(1)}, u32[]{:S(2)}, u32[]{:S(2)}) collective-permute-start(bf16[192,3072]{1,0:T(8,128)(2,1)S(1)} %collective-permute-done.5), channel_id=1, source_target_pairs={{0,7},{1,0},{2,1},{3,2},{4,3},{5,4},{6,5},{7,6},{8,15},{9,8},{10,9... | collective-permute-start | bytes 3538952 | tf_op jit(solution)/shard_map/ppermute | solution.py:32
  97.6 15.6 %collective-permute-start.8 = (bf16[192,3072]{1,0:T(8,128)(2,1)S(1)}, bf16[192,3072]{1,0:T(8,128)(2,1)S(1)}, u32[]{:S(2)}, u32[]{:S(2)}) collective-permute-start(bf16[192,3072]{1,0:T(8,128)(2,1)S(1)} %collective-permute-done.6), channel_id=1, source_target_pairs={{0,1},{1,2},{2,3},{3,4},{4,5},{5,6},{6,7},{7,0},{8,9},{9,10},{10,1... | collective-permute-start | bytes 3538952 | tf_op jit(solution)/shard_map/ppermute | solution.py:27
  140.0 5.8 %collective-permute-start.9 = (bf16[15,1536]{1,0:T(8,128)(2,1)S(1)}, bf16[15,1536]{1,0:T(8,128)(2,1)S(1)}, u32[]{:S(2)}, u32[]{:S(2)}) collective-permute-start(bf16[15,1536]{1,0:T(8,128)(2,1)S(1)} %get-tuple-element.50), channel_id=1, source_target_pairs={{0,8},{8,16},{16,24},{24,32},{32,40},{40,48},{48,56},{56,64},{64,7... | collective-permute-start | bytes 138248 | tf_op jit(solution)/shard_map/ppermute | solution.py:42
  144.4 6.0 %collective-permute-start.10 = (bf16[15,1536]{1,0:T(8,128)(2,1)S(1)}, bf16[15,1536]{1,0:T(8,128)(2,1)S(1)}, u32[]{:S(2)}, u32[]{:S(2)}) collective-permute-start(bf16[15,1536]{1,0:T(8,128)(2,1)S(1)} %get-tuple-element.49), channel_id=1, source_target_pairs={{8,0},{16,8},{24,16},{32,24},{40,32},{48,40},{56,48},{64,56},{72,6... | collective-permute-start | bytes 138248 | tf_op jit(solution)/shard_map/ppermute | solution.py:42
  186.3 238.8 %collective-permute-start.11 = (bf16[128,1536]{1,0:T(8,128)(2,1)S(1)}, bf16[128,1536]{1,0:T(8,128)(2,1)S(1)}, u32[]{:S(2)}, u32[]{:S(2)}) collective-permute-start(bf16[128,1536]{1,0:T(8,128)(2,1)S(1)} %get-tuple-element.47), channel_id=1, source_target_pairs={{8,0},{16,8},{24,16},{32,24},{40,32},{48,40},{56,48},{64,56},{72,6... | collective-permute-start | bytes 1179656 | tf_op jit(solution)/shard_map/ppermute | solution.py:42
  187.6 237.5 %collective-permute-start.12 = (bf16[128,1536]{1,0:T(8,128)(2,1)S(1)}, bf16[128,1536]{1,0:T(8,128)(2,1)S(1)}, u32[]{:S(2)}, u32[]{:S(2)}) collective-permute-start(bf16[128,1536]{1,0:T(8,128)(2,1)S(1)} %get-tuple-element.48), channel_id=1, source_target_pairs={{0,8},{8,16},{16,24},{24,32},{32,40},{40,48},{48,56},{56,64},{64,7... | collective-permute-start | bytes 1179656 | tf_op jit(solution)/shard_map/ppermute | solution.py:42
  420.9 8.5 %collective-permute-start.13 = (bf16[8,3072]{1,0:T(8,128)(2,1)S(1)}, bf16[8,3072]{1,0:T(8,128)(2,1)S(1)}, u32[]{:S(2)}, u32[]{:S(2)}) collective-permute-start(bf16[8,3072]{1,0:T(8,128)(2,1)S(1)} %fusion), channel_id=1, source_target_pairs={{0,1},{1,2},{2,3},{3,4},{4,5},{5,6},{6,7},{8,9},{9,10},{10,11},{11... | collective-permute-start | bytes 147464
  422.8 6.6 %collective-permute-start.14 = (bf16[6,3072]{1,0:T(8,128)(2,1)S(1)}, bf16[6,3072]{1,0:T(8,128)(2,1)S(1)}, u32[]{:S(2)}, u32[]{:S(2)}) collective-permute-start(bf16[6,3072]{1,0:T(8,128)(2,1)S(1)} %slice.684), channel_id=1, source_target_pairs={{0,2},{1,3},{2,4},{3,5},{4,6},{5,7},{8,10},{9,11},{10,12},{11,13},... | collective-permute-start | bytes 110600
  (59 other events, 476.7 us)
Sparse Core Ops, SparseCore 0:
  15.8 75.3 all-gather.1
Sparse Core Ops, SparseCore 1:
  170.3 235.9 reduce-scatter.3
